TPU v7x, 32 devices: a whole 2x2x4 slice. The times are simulated.
32 devices in a mesh: seq: 8 (over z, y), blk: 2 (over x), grp: 2 (over core).
Axes of the slice: x: 2, y: 2, z: 4, core: 2. Of those that a mesh axis runs over, the one named last changes fastest.
Arguments:
- activations: bfloat16 [8192, 2048], P('seq', 'blk'), may hold values from -23 to 23
- cotangent: bfloat16 [8192, 1024], P('seq'), may hold values from -0.09375 to 0.09375
- factor: float32 [2048, 1024], P('blk', ('seq', 'grp')), may hold values from -0.3 to 1.7
Outputs:
- new_factor: float32 [2048, 1024], P('blk', ('seq', 'grp'))
- direction: float32 [2048, 1024], P('blk', ('seq', 'grp'))
All inputs are finite; a program needn't handle non-finite values.
Results may differ from a plain program's by a relative error of at most 0.007.
Values may be sent and summed in bfloat16 or wider, within the bound.
A program may use at most 64 MiB of HBM per device.

v0:
```python
import jax
import jax.numpy as jnp
from jax import lax
from jax.sharding import PartitionSpec as P

damping = 0.25
step_size = 0.4


def strided_columns(matrix, seq_count, grp_count, grp_index):
    height = matrix.shape[0]
    narrow = matrix.shape[1] // (seq_count * grp_count)
    shaped = matrix.reshape(height, seq_count, grp_count, narrow)
    picked = lax.dynamic_slice_in_dim(shaped, grp_index, 1, 2)
    return picked.reshape(height, seq_count * narrow)


def on_device(activations, cotangent, factor):
    seq_count = lax.axis_size("seq")
    grp_count = lax.axis_size("grp")
    seq_index = lax.axis_index("seq")
    grp_index = lax.axis_index("grp")
    width = factor.shape[0]
    owned = factor.shape[1]
    total_tokens = activations.shape[0] * seq_count
    tokens_first = (((0,), (0,)), ((), ()))
    factor_low = factor.astype(jnp.bfloat16)
    whole_factor = lax.all_gather(factor_low, ("seq", "grp"), axis=1, tiled=True)
    whitened = jnp.dot(activations, whole_factor, preferred_element_type=jnp.float32).astype(
        jnp.bfloat16
    )
    chosen = strided_columns(whitened, seq_count, grp_count, grp_index)
    out_columns = strided_columns(cotangent, seq_count, grp_count, grp_index)
    piece = out_columns
    gradient_rows = lax.psum_scatter(
        lax.dot_general(piece, activations, tokens_first, preferred_element_type=jnp.float32),
        "seq",
        scatter_dimension=0,
        tiled=True,
    ).astype(jnp.bfloat16)
    piece = chosen
    gram_rows = lax.psum_scatter(
        lax.dot_general(piece, whitened, tokens_first, preferred_element_type=jnp.float32),
        "seq",
        scatter_dimension=0,
        tiled=True,
    )
    cross_rows = lax.dot_general(
        factor_low, whole_factor, tokens_first, preferred_element_type=jnp.float32
    )
    position = seq_index * grp_count + grp_index
    column_ids = position * owned + jnp.arange(owned, dtype=jnp.int32)
    identity_rows = (jnp.arange(width, dtype=jnp.int32)[None, :] == column_ids[:, None]).astype(
        jnp.float32
    )
    curvature = (gram_rows / total_tokens + damping * cross_rows - identity_rows).astype(
        jnp.bfloat16
    )
    update = lax.dot_general(
        whole_factor, curvature, (((1,), (1,)), ((), ())), preferred_element_type=jnp.float32
    )
    new_factor = factor - 0.5 * step_size * update
    half = lax.dot_general(
        whole_factor, gradient_rows, (((0,), (1,)), ((), ())), preferred_element_type=jnp.float32
    ).astype(jnp.bfloat16)
    direction = jnp.dot(whole_factor, half, preferred_element_type=jnp.float32)
    return (new_factor, direction)


def solution(mesh):
    placed = (P("seq", "blk"), P("seq", None), P("blk", ("seq", "grp")))
    return jax.shard_map(
        on_device,
        mesh=mesh,
        in_specs=placed,
        out_specs=(P("blk", ("seq", "grp")), P("blk", ("seq", "grp"))),
        check_vma=False,
    )
```

profile of v0, /device:TPU:0, one launch (start us, length us, event | category | flops | bytes accessed | tf_op | source)
XLA Modules:
  0.0 210.9 jit_solution(4081033319611897926)
XLA Ops:
  7.2 0.0 copy-start
  7.2 0.0 all-gather.2.cloned.1.call-start
  7.2 1.8 convert_element_type.19
  9.0 0.0 all-gather.2.cloned.1.call-update
  9.0 0.0 reduce-scatter.5.cloned.1.call-start
  9.1 3.9 %copy.5 = bf16[1024,1024]{0,1:T(8,128)(2,1)} copy(bf16[1024,1024]{1,0:T(8,128)(2,1)} %param.4) | data formatting | bytes 4194304 | tf_op args[1]
  13.0 41.9 %all-gather.2.cloned.1.call-done = bf16[1024,1024]{0,1:T(8,128)(2,1)} async-done(((bf16[1024,64]{0,1:T(8,128)(2,1)}), bf16[1024,1024]{0,1:T(8,128)(2,1)}) %all-gather.2.cloned.1.call-update) | async-done | bytes 2097168 | tf_op jit(solution)/shard_map/all_gather | solution.py:28
  54.9 0.0 copy-done
  54.9 0.0 copy-start.1
  54.9 4.1 %convolution_convert_fusion = bf16[1024,1024]{0,1:T(8,128)(2,1)S(1)} fusion(bf16[1024,1024]{1,0:T(8,128)(2,1)S(1)} %copy-done, bf16[1024,1024]{0,1:T(8,128)(2,1)} %all-gather.2.cloned.1.call-done), kind=kOutput, calls=%fused_computation | convolution fusion | flops 2148532224 | bytes 6291456 | tf_op jit(solution)/shard_map/dot_general | solution.py:29
  59.0 0.0 copy-start.3
  59.0 0.0 copy-done.1
  59.0 0.2 constant_dynamic-slice_fusion
  59.3 1.0 copy-done.3
  60.3 2.6 %fusion.17 = f32[512,1024]{1,0:T(8,128)} fusion(bf16[1024,512]{0,1:T(8,128)(2,1)S(1)} %bitcast.22, bf16[1024,1024]{1,0:T(8,128)(2,1)S(1)} %copy-done), kind=kOutput, calls=%fused_computation.24 | convolution fusion | flops 1073741824 | bytes 5242880 | tf_op jit(solution)/shard_map/dot_general | solution.py:36
  62.9 0.0 reduce-scatter.5.cloned.1.call-update
  62.9 0.0 reduce-scatter.3.cloned.1.call-start
  63.0 4.2 %fusion.16 = f32[512,1024]{1,0:T(8,128)} fusion(bf16[1024,512]{0,1:T(8,128)(2,1)S(1)} %bitcast.21, bf16[1024,1024]{0,1:T(8,128)(2,1)} %copy-done.3), kind=kOutput, calls=%fused_computation.23 | convolution fusion | flops 1073741824 | bytes 5242880 | tf_op jit(solution)/shard_map/dot_general | solution.py:43
  67.2 0.0 reduce-scatter.3.cloned.1.call-update
  67.2 0.0 copy-start.2
  67.2 62.4 %reduce-scatter.5.cloned.1.call-done = f32[64,1024]{1,0:T(8,128)} async-done(((f32[512,1024]{1,0:T(8,128)}), f32[64,1024]{1,0:T(8,128)}) %reduce-scatter.5.cloned.1.call-update) | async-done | bytes 262160 | tf_op jit(solution)/shard_map/reduce_scatter | solution.py:35
  129.7 4.1 %convolution_bitcast_fusion = f32[1024,64]{0,1:T(8,128)} fusion(bf16[1024,1024]{0,1:T(8,128)(2,1)} %all-gather.2.cloned.1.call-done, f32[64,1024]{1,0:T(8,128)} %reduce-scatter.5.cloned.1.call-done), kind=kOutput, calls=%fused_computation.7 | convolution fusion | flops 268566528 | bytes 2621440 | tf_op jit(solution)/shard_map/dot_general | solution.py:66
  133.8 66.4 %reduce-scatter.3.cloned.1.call-done = f32[64,1024]{1,0:T(8,128)} async-done(((f32[512,1024]{1,0:T(8,128)}), f32[64,1024]{1,0:T(8,128)}) %reduce-scatter.3.cloned.1.call-update) | async-done | bytes 262160 | tf_op jit(solution)/shard_map/reduce_scatter | solution.py:42
  200.2 0.0 copy-done.2
  200.2 4.2 %fusion.1 = f32[1024,64]{0,1:T(8,128)} fusion(f32[1024,64]{0,1:T(8,128)S(1)} %copy-done.2, bf16[1024,1024]{0,1:T(8,128)(2,1)} %all-gather.2.cloned.1.call-done, f32[64,1024]{1,0:T(8,128)} %reduce-scatter.3.cloned.1.call-done, s32[64]{0:T(128)S(1)} %iota_add_fusion), kind=kOutput, calls=%fused_computation.3 | convolution fusion | flops 269090816 | bytes 2883840 | tf_op jit(solution)/shard_map/dot_general | solution.py:59
  (1 shorter events, 0.0 us)
Async XLA Ops:
  7.2 47.7 %copy-start = (bf16[1024,1024]{1,0:T(8,128)(2,1)S(1)}, bf16[1024,1024]{1,0:T(8,128)(2,1)}, u32[]{:S(2)}) copy-start(bf16[1024,1024]{1,0:T(8,128)(2,1)} %param.3) | copy-start | bytes 6291460
  7.2 47.7 %all-gather.2.cloned.1.call-start = ((), (), s32[]{:S(2)}) async-start(), calls=%async_computation.2 | async-start | bytes 2228224 | tf_op jit(solution)/shard_map/all_gather | solution.py:28
  9.0 120.6 %reduce-scatter.5.cloned.1.call-start = ((), (), s32[]{:S(2)}) async-start(), calls=%async_computation.4 | async-start | bytes 2359296 | tf_op jit(solution)/shard_map/reduce_scatter | solution.py:35
  54.9 4.1 %copy-start.1 = (bf16[1024,1024]{0,1:T(8,128)(2,1)S(1)}, bf16[1024,1024]{0,1:T(8,128)(2,1)}, u32[]{:S(2)}) copy-start(bf16[1024,1024]{0,1:T(8,128)(2,1)} %copy.5) | copy-start | bytes 6291460
  59.0 1.3 copy-start.3
  62.9 137.2 %reduce-scatter.3.cloned.1.call-start = ((), (), s32[]{:S(2)}) async-start(), calls=%async_computation.3 | async-start | bytes 2359296 | tf_op jit(solution)/shard_map/reduce_scatter | solution.py:42
  67.2 132.9 %copy-start.2 = (f32[1024,64]{0,1:T(8,128)S(1)}, f32[1024,64]{0,1:T(8,128)}, u32[]{:S(2)}) copy-start(f32[1024,64]{0,1:T(8,128)} %param.5) | copy-start | bytes 786436
Sparse Core Ops, SparseCore 0:
  10.7 44.0 all-gather.1
  63.1 66.5 reduce-scatter.4
  133.2 66.9 reduce-scatter.2
where the time goes:
time: 211 us
  waiting for transfers between devices  171 us (81%)
  matrix products  19.2 us (9%)
  between operations  13.8 us (7%)
  local copies, waits for them, and re-layouts  5.23 us (2%)
    reduce_scatter x1, waiting for transfers between devices, on_device(): lax.psum_scatter(lax.dot_general(piece, whitened, tokens_first, preferred...  66.4 us
    reduce_scatter x1, waiting for transfers between devices, on_device(): lax.psum_scatter(lax.dot_general(piece, activations, tokens_first, prefer...  62.4 us
    all_gather x1, waiting for transfers between devices, on_device(): lax.all_gather(factor_low, ('seq', 'grp'), axis=1, tiled=True)  41.9 us
    unnamed x9, local copies, waits for them, and re-layouts  5 us
  transfers between devices with their start and end apart: 3, of which 3 were waited for; matrix products, arithmetic and copies ran while one was open for 6% of the time, Pallas kernels for 0%

commit v1 on v0

v1 whole, which is shorter than its diff:
```python
import functools

import jax
import jax.numpy as jnp
from jax import lax
from jax.experimental import pallas as pl
from jax.experimental.pallas import tpu as pltpu
from jax.sharding import PartitionSpec as P

damping = 0.25
step_size = 0.4

NT = (((1,), (1,)), ((), ()))
NN = (((1,), (0,)), ((), ()))
MESH = pl.DeviceIdType.MESH


def dot(left, right, dims):
    return lax.dot_general(left, right, dims, preferred_element_type=jnp.float32)


def kernel(
    n, grps, total_tokens,
    a_hbm, c_hbm, f_ref, new_ref, dir_ref,
    a, c, ct, kt, wt, send_buf, recv_buf,
    local_sem, ag_send, ag_recv, pair_send, pair_recv, rs_send, rs_recv,
):
    hops = n // 2
    lines = 4 if n % 4 == 0 else 1
    per_line = n // lines
    width, owned = f_ref.shape
    half = width // 2
    me = lax.axis_index("seq")
    grp = lax.axis_index("grp")

    my_y, my_z = lax.rem(me, per_line), lax.div(me, per_line)
    pos = my_y * lines + my_z + lax.rem(my_y, 2) * (lines - 1 - 2 * my_z)

    def at(offset):
        place = lax.rem(pos + offset + n, n)
        y, t = lax.div(place, lines), lax.rem(place, lines)
        return (t + lax.rem(y, 2) * (lines - 1 - 2 * t)) * per_line + y

    neighbour = (at(1), at(-1))
    sign = (1, -1)
    partners = [lax.rem(grp + j, grps) for j in range(1, grps)]

    def rows(offset, g=None):
        g = grp if g is None else g
        return pl.ds(pl.multiple_of((at(offset) * grps + g) * owned, owned), owned)

    def pair_rows(offset):
        return pl.ds(pl.multiple_of(at(offset) * grps * owned, grps * owned), grps * owned)

    def cols(h):
        return pl.ds(h * half, half)

    load_a = pltpu.make_async_copy(a_hbm, a, local_sem.at[0])
    load_c = pltpu.make_async_copy(c_hbm, c, local_sem.at[1])
    load_c.start()
    load_a.start()

    barrier = pltpu.get_barrier_semaphore()
    for d in range(2):
        pl.semaphore_signal(barrier, inc=1, device_id={"seq": neighbour[d]}, device_id_type=MESH)
    for other in partners:
        pl.semaphore_signal(barrier, inc=1, device_id={"grp": other}, device_id_type=MESH)
    kt[rows(0), :] = jnp.transpose(f_ref[...]).astype(jnp.bfloat16)
    pl.semaphore_wait(barrier, 2 + len(partners))

    started = []

    def ag_copy(d, k, h, offset):
        piece = kt.at[rows(offset), cols(h)]
        return pltpu.make_async_remote_copy(
            src_ref=piece, dst_ref=piece,
            send_sem=ag_send.at[d, k - 1, h], recv_sem=ag_recv.at[d, k - 1, h],
            device_id={"seq": neighbour[d]}, device_id_type=MESH,
        )

    def ag_start(d, k, h):
        if k == hops and h != d:
            return
        copy = ag_copy(d, k, h, -sign[d] * (k - 1))
        copy.start()
        started.append(copy)

    def pair_copy(d, k, h, j, offset, g):
        piece = kt.at[rows(offset, g), cols(h)]
        return pltpu.make_async_remote_copy(
            src_ref=piece, dst_ref=piece,
            send_sem=pair_send.at[d, k, h, j], recv_sem=pair_recv.at[d, k, h, j],
            device_id={"grp": partners[j]}, device_id_type=MESH,
        )

    def pair_start(d, k, h):
        for j in range(len(partners)):
            copy = pair_copy(d, k, h, j, -sign[d] * k, grp)
            copy.start()
            started.append(copy)

    def pair_wait(d, k, h):
        for j in range(len(partners)):
            source = lax.rem(grp - (j + 1) + grps, grps)
            pair_copy(d, k, h, j, -sign[d] * k, source).wait_recv()

    def ag_hop(k):
        for h in range(2):
            for d in range(2):
                e = h if d == 0 else 1 - h
                if k == hops and e != d:
                    continue
                ag_copy(d, k, e, -sign[d] * k).wait_recv()
                if k < hops:
                    ag_start(d, k + 1, e)
                pair_start(d, k, e)

    def whiten(k):
        offsets = (0,) if k == 0 else ((hops,) if k == hops else (-k, k))
        for d in range(2):
            for h in range(2):
                if (k == 0 and d == 1) or (k == hops and h != d):
                    continue
                pair_wait(d, k, h)
        lhs = [kt[pair_rows(o), :] for o in offsets]
        lhs = lhs[0] if len(lhs) == 1 else jnp.concatenate(lhs, 0)
        out = dot(lhs, a[...], NT).astype(jnp.bfloat16)
        for i, o in enumerate(offsets):
            wt[pair_rows(o), :] = out[i * grps * owned:(i + 1) * grps * owned]

    def rs_copy(r, d, k, h):
        return pltpu.make_async_remote_copy(
            src_ref=send_buf.at[r, d, k - 1, :, cols(h)], dst_ref=recv_buf.at[r, d, k - 1, :, cols(h)],
            send_sem=rs_send.at[r, d, k - 1, h], recv_sem=rs_recv.at[r, d, k - 1, h],
            device_id={"seq": neighbour[d]}, device_id_type=MESH,
        )

    def rs_hop(r, k, partial):
        far = hops + 1 - k
        if k == 1:
            own = partial((far,))[0]
        else:
            own = partial((far, -far))
        for h in range(2):
            for d in range(2):
                e = h if d == 0 else 1 - h
                if k == 1:
                    if e != d:
                        continue
                    value = own[:, e * half:(e + 1) * half]
                else:
                    value = own[d][:, e * half:(e + 1) * half]
                    if k > 2 or e == d:
                        rs_copy(r, d, k - 1, e).wait_recv()
                        value = value + recv_buf[r, d, k - 2, :, cols(e)].astype(jnp.float32)
                send_buf[r, d, k - 1, :, cols(e)] = value.astype(jnp.bfloat16)
                copy = rs_copy(r, d, k, e)
                copy.start()
                started.append(copy)

    def rs_last(r, own):
        parts = []
        for e in range(2):
            value = own[:, e * half:(e + 1) * half]
            for d in range(2):
                rs_copy(r, d, hops, e).wait_recv()
                value = value + recv_buf[r, d, hops - 1, :, cols(e)].astype(jnp.float32)
            parts.append(value)
        return jnp.concatenate(parts, 1)

    def rows_of(ref, offsets):
        taken = [ref[rows(o), :] for o in offsets]
        return taken[0] if len(taken) == 1 else jnp.concatenate(taken, 0)

    def split(value, offsets):
        return [value[i * owned:(i + 1) * owned] for i in range(len(offsets))]

    def grad_part(offsets):
        return split(dot(rows_of(ct, offsets), a[...], NN), offsets)

    def gram_part(offsets):
        return split(dot(rows_of(wt, offsets), wt[...], NT), offsets)

    for h in range(2):
        for d in range(2):
            ag_start(d, 1, h if d == 0 else 1 - h)
    for h in range(2):
        pair_start(0, 0, h)

    load_c.wait()
    ct[...] = jnp.transpose(c[...])
    load_a.wait()
    rs_hop(0, 1, grad_part)
    whiten(0)
    early = hops // 2
    for k in range(1, hops + 1):
        ag_hop(k)
        if 2 <= k + 1 <= early:
            rs_hop(0, k + 1, grad_part)
        if k < hops:
            whiten(k)
    whiten(hops)
    rs_hop(1, 1, gram_part)
    cross = dot(kt[rows(0), :], kt[...], NT)
    for k in range(early + 1, hops + 1):
        rs_hop(0, k, grad_part)
        if 2 <= k - early + 1 <= hops:
            rs_hop(1, k - early + 1, gram_part)
    for k in range(hops - early + 2, hops + 1):
        rs_hop(1, k, gram_part)
    gradient = rs_last(0, grad_part((0,))[0]).astype(jnp.bfloat16)
    halved = dot(gradient, kt[...], NT).astype(jnp.bfloat16)
    dir_ref[...] = jnp.transpose(dot(halved, kt[...], NN))
    first = (me * grps + grp) * owned
    line = lax.broadcasted_iota(jnp.int32, (owned, width), 0) + first
    identity = (line == lax.broadcasted_iota(jnp.int32, (owned, width), 1)).astype(jnp.float32)
    own_gram = gram_part((0,))[0]
    gram = rs_last(1, own_gram)
    curvature = (gram / total_tokens + damping * cross - identity).astype(jnp.bfloat16)
    update = dot(curvature, kt[...], NN)
    new_ref[...] = f_ref[...] - 0.5 * step_size * jnp.transpose(update)
    for copy in started:
        copy.wait_send()


def on_device(n, grps, activations, cotangent, factor):
    tokens, width = activations.shape
    out_width = cotangent.shape[1]
    owned = factor.shape[1]
    hops = n // 2
    low = jnp.bfloat16
    pairs = max(grps - 1, 1)
    dma = pltpu.SemaphoreType.DMA
    vmem = pl.BlockSpec(memory_space=pltpu.VMEM)
    flops = 2 * tokens * width * (width + width // grps + out_width // grps)
    return pl.pallas_call(
        functools.partial(kernel, n, grps, tokens * n),
        out_shape=(
            jax.ShapeDtypeStruct((width, owned), jnp.float32),
            jax.ShapeDtypeStruct((width, owned), jnp.float32),
        ),
        in_specs=[pl.BlockSpec(memory_space=pl.ANY)] * 2 + [vmem],
        out_specs=(vmem, vmem),
        scratch_shapes=[
            pltpu.VMEM((tokens, width), low),
            pltpu.VMEM((tokens, out_width), low),
            pltpu.VMEM((out_width, tokens), low),
            pltpu.VMEM((width, width), low),
            pltpu.VMEM((width, tokens), low),
            pltpu.VMEM((2, 2, hops, owned, width), low),
            pltpu.VMEM((2, 2, hops, owned, width), low),
            dma((2,)),
            dma((2, hops, 2)),
            dma((2, hops, 2)),
            dma((2, hops + 1, 2, pairs)),
            dma((2, hops + 1, 2, pairs)),
            dma((2, 2, hops, 2)),
            dma((2, 2, hops, 2)),
        ],
        compiler_params=pltpu.CompilerParams(
            collective_id=0, has_side_effects=True, vmem_limit_bytes=48 * 1024 * 1024
        ),
        cost_estimate=pl.CostEstimate(
            flops=flops, bytes_accessed=4 * tokens * width, transcendentals=0
        ),
    )(activations, cotangent, factor)


def solution(mesh):
    placed = (P("seq", "blk"), P("seq", None), P("blk", ("seq", "grp")))
    return jax.shard_map(
        functools.partial(on_device, mesh.shape["seq"], mesh.shape["grp"]),
        mesh=mesh,
        in_specs=placed,
        out_specs=(P("blk", ("seq", "grp")), P("blk", ("seq", "grp"))),
        check_vma=False,
    )
```

time: 211 us -> 51.2 us (0.24)
  waiting for transfers between devices: 171 us -> 0 us
  Pallas kernels: 0 us -> 44.2 us
  matrix products: 19.2 us -> 0 us
  between operations: 13.8 us -> 0.66 us
    reduce_scatter x2 -> x0, waiting for transfers between devices: 129 us -> none  [the longest x1 66.4 us: on_device(): lax.psum_scatter(lax.dot_general(piece, whitened, tokens_first, preferred...]
    pallas_call x0 -> x1, Pallas kernels: none -> 44.2 us  [on_device(): pl.pallas_call(functools.partial(kernel, n, grps, tokens * n), out_shape=...]
    all_gather x1 -> x0, waiting for transfers between devices: 41.9 us -> none  [on_device(): lax.all_gather(factor_low, ('seq', 'grp'), axis=1, tiled=True)]
    dot_general x5 -> x0, matrix products: 19.2 us -> none  [the longest x1 4.2 us: on_device(): lax.dot_general(piece, whitened, tokens_first, preferred_element_type=jnp...]
    unnamed x9 -> x5, local copies, waits for them, and re-layouts: 5 us -> 4.32 us
  transfers between devices with their start and end apart: 3 -> 0, of which waited for: 3 -> 0; matrix products, arithmetic and copies ran while one was open for 6% -> 0% of each run, Pallas kernels for 0% -> 0%
where the time goes in v1:
time: 51.2 us; the launch traced here: 51 us
  Pallas kernels  44.2 us (86%)
  local copies, waits for them, and re-layouts  6.1 us (12%)
  between operations  0.66 us (1%)
    pallas_call x1, Pallas kernels, on_device(): pl.pallas_call(functools.partial(kernel, n, grps, tokens * n), out_shape=...  44.2 us
    unnamed x5, local copies, waits for them, and re-layouts  4.32 us
    pallas_call x2, local copies, waits for them, and re-layouts, on_device(): pl.pallas_call(functools.partial(kernel, n, grps, tokens * n), out_shape=...  1.77 us

profile of v1, /device:TPU:0, one launch (start us, length us, event | category | flops | bytes accessed | tf_op | source)
XLA Modules:
  0.0 51.0 jit_solution(14804587221512487609)
XLA Ops:
  0.6 1.1 %copy.5.f_ref = f32[1024,64]{1,0:T(8,128)S(1)} copy(f32[1024,64]{0,1:T(8,128)} %param.5) | data formatting | bytes 524288 | tf_op args[2]
  1.8 0.0 copy-start
  1.8 1.6 %copy-done = bf16[1024,1024]{1,0:T(8,128)(2,1)S(1)} copy-done((bf16[1024,1024]{1,0:T(8,128)(2,1)S(1)}, bf16[1024,1024]{1,0:T(8,128)(2,1)}, u32[]{:S(2)}) %copy-start) | copy-done | bytes 2097176
  3.4 0.0 copy-start.1
  3.4 1.6 %copy-done.1 = bf16[1024,1024]{1,0:T(8,128)(2,1)S(1)} copy-done((bf16[1024,1024]{1,0:T(8,128)(2,1)S(1)}, bf16[1024,1024]{1,0:T(8,128)(2,1)}, u32[]{:S(2)}) %copy-start.1) | copy-done | bytes 2097176
  5.0 44.2 %shard_map.50 = (f32[1024,64]{1,0:T(8,128)S(1)}, f32[1024,64]{1,0:T(8,128)S(1)}) custom-call(bf16[1024,1024]{1,0:T(8,128)(2,1)S(1)} %copy-done, bf16[1024,1024]{1,0:T(8,128)(2,1)S(1)} %copy-done.1, f32[1024,64]{1,0:T(8,128)S(1)} %copy.5.f_ref), custom_call_target="tpu_custom_call" | custom-call | flops 4294967296 | bytes 4194304 | tf_op jit(solution)/shard_map/pallas_call | solution.py:236
  49.2 0.9 %copy.6 = f32[1024,64]{0,1:T(8,128)} copy(f32[1024,64]{1,0:T(8,128)S(1)} %get-tuple-element.2) | data formatting | bytes 524288 | tf_op jit(solution)/shard_map/pallas_call | solution.py:236
  50.1 0.9 %copy.7 = f32[1024,64]{0,1:T(8,128)} copy(f32[1024,64]{1,0:T(8,128)S(1)} %get-tuple-element.3) | data formatting | bytes 524288 | tf_op jit(solution)/shard_map/pallas_call | solution.py:236
Async XLA Ops:
  1.8 1.6 %copy-start = (bf16[1024,1024]{1,0:T(8,128)(2,1)S(1)}, bf16[1024,1024]{1,0:T(8,128)(2,1)}, u32[]{:S(2)}) copy-start(bf16[1024,1024]{1,0:T(8,128)(2,1)} %a_hbm.1) | copy-start | bytes 6291460
  3.4 1.6 %copy-start.1 = (bf16[1024,1024]{1,0:T(8,128)(2,1)S(1)}, bf16[1024,1024]{1,0:T(8,128)(2,1)}, u32[]{:S(2)}) copy-start(bf16[1024,1024]{1,0:T(8,128)(2,1)} %c_hbm.1) | copy-start | bytes 6291460

commit v2 on v1

--- a/solution.py
+++ b/solution.py
@@ -28,7 +28,7 @@
     hops = n // 2
     lines = 4 if n % 4 == 0 else 1
     per_line = n // lines
-    width, owned = f_ref.shape
+    owned, width = f_ref.shape
     half = width // 2
     me = lax.axis_index("seq")
     grp = lax.axis_index("grp")
@@ -65,7 +65,7 @@
         pl.semaphore_signal(barrier, inc=1, device_id={"seq": neighbour[d]}, device_id_type=MESH)
     for other in partners:
         pl.semaphore_signal(barrier, inc=1, device_id={"grp": other}, device_id_type=MESH)
-    kt[rows(0), :] = jnp.transpose(f_ref[...]).astype(jnp.bfloat16)
+    kt[rows(0), :] = f_ref[...].astype(jnp.bfloat16)
     pl.semaphore_wait(barrier, 2 + len(partners))
 
     started = []
@@ -130,7 +130,7 @@
 
     def rs_copy(r, d, k, h):
         return pltpu.make_async_remote_copy(
-            src_ref=send_buf.at[r, d, k - 1, :, cols(h)], dst_ref=recv_buf.at[r, d, k - 1, :, cols(h)],
+            src_ref=send_buf.at[r, d, k - 1, h], dst_ref=recv_buf.at[r, d, k - 1, h],
             send_sem=rs_send.at[r, d, k - 1, h], recv_sem=rs_recv.at[r, d, k - 1, h],
             device_id={"seq": neighbour[d]}, device_id_type=MESH,
         )
@@ -152,8 +152,8 @@
                     value = own[d][:, e * half:(e + 1) * half]
                     if k > 2 or e == d:
                         rs_copy(r, d, k - 1, e).wait_recv()
-                        value = value + recv_buf[r, d, k - 2, :, cols(e)].astype(jnp.float32)
-                send_buf[r, d, k - 1, :, cols(e)] = value.astype(jnp.bfloat16)
+                        value = value + recv_buf[r, d, k - 2, e].astype(jnp.float32)
+                send_buf[r, d, k - 1, e] = value.astype(jnp.bfloat16)
                 copy = rs_copy(r, d, k, e)
                 copy.start()
                 started.append(copy)
@@ -164,7 +164,7 @@
             value = own[:, e * half:(e + 1) * half]
             for d in range(2):
                 rs_copy(r, d, hops, e).wait_recv()
-                value = value + recv_buf[r, d, hops - 1, :, cols(e)].astype(jnp.float32)
+                value = value + recv_buf[r, d, hops - 1, e].astype(jnp.float32)
             parts.append(value)
         return jnp.concatenate(parts, 1)
 
@@ -192,7 +192,7 @@
     load_a.wait()
     rs_hop(0, 1, grad_part)
     whiten(0)
-    early = hops // 2
+    early = hops
     for k in range(1, hops + 1):
         ag_hop(k)
         if 2 <= k + 1 <= early:
@@ -210,7 +210,7 @@
         rs_hop(1, k, gram_part)
     gradient = rs_last(0, grad_part((0,))[0]).astype(jnp.bfloat16)
     halved = dot(gradient, kt[...], NT).astype(jnp.bfloat16)
-    dir_ref[...] = jnp.transpose(dot(halved, kt[...], NN))
+    dir_ref[...] = dot(halved, kt[...], NN)
     first = (me * grps + grp) * owned
     line = lax.broadcasted_iota(jnp.int32, (owned, width), 0) + first
     identity = (line == lax.broadcasted_iota(jnp.int32, (owned, width), 1)).astype(jnp.float32)
@@ -218,7 +218,7 @@
     gram = rs_last(1, own_gram)
     curvature = (gram / total_tokens + damping * cross - identity).astype(jnp.bfloat16)
     update = dot(curvature, kt[...], NN)
-    new_ref[...] = f_ref[...] - 0.5 * step_size * jnp.transpose(update)
+    new_ref[...] = f_ref[...] - 0.5 * step_size * update
     for copy in started:
         copy.wait_send()
 
@@ -233,11 +233,11 @@
     dma = pltpu.SemaphoreType.DMA
     vmem = pl.BlockSpec(memory_space=pltpu.VMEM)
     flops = 2 * tokens * width * (width + width // grps + out_width // grps)
-    return pl.pallas_call(
+    new_rows, direction_rows = pl.pallas_call(
         functools.partial(kernel, n, grps, tokens * n),
         out_shape=(
-            jax.ShapeDtypeStruct((width, owned), jnp.float32),
-            jax.ShapeDtypeStruct((width, owned), jnp.float32),
+            jax.ShapeDtypeStruct((owned, width), jnp.float32),
+            jax.ShapeDtypeStruct((owned, width), jnp.float32),
         ),
         in_specs=[pl.BlockSpec(memory_space=pl.ANY)] * 2 + [vmem],
         out_specs=(vmem, vmem),
@@ -247,8 +247,8 @@
             pltpu.VMEM((out_width, tokens), low),
             pltpu.VMEM((width, width), low),
             pltpu.VMEM((width, tokens), low),
-            pltpu.VMEM((2, 2, hops, owned, width), low),
-            pltpu.VMEM((2, 2, hops, owned, width), low),
+            pltpu.VMEM((2, 2, hops, 2, owned, width // 2), low),
+            pltpu.VMEM((2, 2, hops, 2, owned, width // 2), low),
             dma((2,)),
             dma((2, hops, 2)),
             dma((2, hops, 2)),
@@ -258,12 +258,13 @@
             dma((2, 2, hops, 2)),
         ],
         compiler_params=pltpu.CompilerParams(
-            collective_id=0, has_side_effects=True, vmem_limit_bytes=48 * 1024 * 1024
+            collective_id=0, has_side_effects=True, vmem_limit_bytes=62 * 1024 * 1024
         ),
         cost_estimate=pl.CostEstimate(
             flops=flops, bytes_accessed=4 * tokens * width, transcendentals=0
         ),
-    )(activations, cotangent, factor)
+    )(activations, cotangent, factor.T)
+    return new_rows.T, direction_rows.T
 
 
 def solution(mesh):

time: 51.2 us -> 49.1 us (0.959)
  local copies, waits for them, and re-layouts: 6.1 us -> 3.34 us
  Pallas kernels: 44.2 us -> 44.9 us
    pallas_call x2 -> x0, local copies, waits for them, and re-layouts: 1.77 us -> none  [on_device(): pl.pallas_call(functools.partial(kernel, n, grps, tokens * n), out_shape=...]
    unnamed x5 -> x2, local copies, waits for them, and re-layouts: 4.32 us -> 3.34 us
    pallas_call x1, Pallas kernels: 44.2 us -> 44.9 us  [on_device(): pl.pallas_call(functools.partial(kernel, n, grps, tokens * n), out_shape=...]
where the time goes in v2:
time: 49.1 us; the launch traced here: 48.9 us
  Pallas kernels  44.9 us (91%)
  local copies, waits for them, and re-layouts  3.34 us (7%)
  between operations  0.64 us (1%)
    pallas_call x1, Pallas kernels, on_device(): pl.pallas_call(functools.partial(kernel, n, grps, tokens * n), out_shape=...  44.9 us
    unnamed x2, local copies, waits for them, and re-layouts  3.34 us

profile of v2, /device:TPU:0, one launch (start us, length us, event | category | flops | bytes accessed | tf_op | source)
XLA Modules:
  0.0 48.9 jit_solution(17806449757833817344)
XLA Ops:
  0.6 44.9 %shard_map.50 = (f32[64,1024]{1,0:T(8,128)}, f32[64,1024]{1,0:T(8,128)}) custom-call(bf16[1024,1024]{1,0:T(8,128)(2,1)} %a_hbm.1, bf16[1024,1024]{1,0:T(8,128)(2,1)} %c_hbm.1, f32[64,1024]{1,0:T(8,128)} %bitcast.5), custom_call_target="tpu_custom_call" | custom-call | flops 4294967296 | bytes 4194304 | tf_op jit(solution)/shard_map/pallas_call | solution.py:236
  45.5 1.7 %copy.7 = f32[1024,64]{0,1:T(8,128)} copy(f32[1024,64]{0,1:T(8,128)} %bitcast.4) | data formatting | bytes 524288
  47.2 1.7 %copy.8 = f32[1024,64]{0,1:T(8,128)} copy(f32[1024,64]{0,1:T(8,128)} %bitcast.3) | data formatting | bytes 524288

commit v3 on v2

--- a/solution.py
+++ b/solution.py
@@ -190,13 +190,13 @@
     load_c.wait()
     ct[...] = jnp.transpose(c[...])
     load_a.wait()
-    rs_hop(0, 1, grad_part)
-    whiten(0)
-    early = hops
+    early = hops - 1
     for k in range(1, hops + 1):
         ag_hop(k)
-        if 2 <= k + 1 <= early:
-            rs_hop(0, k + 1, grad_part)
+        if k <= early:
+            rs_hop(0, k, grad_part)
+        if k == 1:
+            whiten(0)
         if k < hops:
             whiten(k)
     whiten(hops)

time: 49.1 us -> 47.4 us (0.965)
  Pallas kernels: 44.9 us -> 43.2 us
    pallas_call x1, Pallas kernels: 44.9 us -> 43.2 us  [on_device(): pl.pallas_call(functools.partial(kernel, n, grps, tokens * n), out_shape=...]
where the time goes in v3:
time: 47.4 us; the launch traced here: 47.1 us
  Pallas kernels  43.2 us (91%)
  local copies, waits for them, and re-layouts  3.34 us (7%)
  between operations  0.64 us (1%)
    pallas_call x1, Pallas kernels, on_device(): pl.pallas_call(functools.partial(kernel, n, grps, tokens * n), out_shape=...  43.2 us
    unnamed x2, local copies, waits for them, and re-layouts  3.34 us

profile of v3, /device:TPU:0, one launch (start us, length us, event | category | flops | bytes accessed | tf_op | source)
XLA Modules:
  0.0 47.1 jit_solution(1253662982308658361)
XLA Ops:
  0.6 43.2 %shard_map.50 = (f32[64,1024]{1,0:T(8,128)}, f32[64,1024]{1,0:T(8,128)}) custom-call(bf16[1024,1024]{1,0:T(8,128)(2,1)} %a_hbm.1, bf16[1024,1024]{1,0:T(8,128)(2,1)} %c_hbm.1, f32[64,1024]{1,0:T(8,128)} %bitcast.5), custom_call_target="tpu_custom_call" | custom-call | flops 4294967296 | bytes 4194304 | tf_op jit(solution)/shard_map/pallas_call | solution.py:236
  43.8 1.7 %copy.7 = f32[1024,64]{0,1:T(8,128)} copy(f32[1024,64]{0,1:T(8,128)} %bitcast.4) | data formatting | bytes 524288
  45.5 1.7 %copy.8 = f32[1024,64]{0,1:T(8,128)} copy(f32[1024,64]{0,1:T(8,128)} %bitcast.3) | data formatting | bytes 524288
